TPU v7x, 32 devices: a whole 2x2x4 slice. The times are simulated.
32 devices in a mesh: batch: 2 (over core), lon: 4 (over y, x), lat: 4 (over z).
Axes of the slice: x: 2, y: 2, z: 4, core: 2. Of those that a mesh axis runs over, the one named last changes fastest.
Arguments:
- imagery: bfloat16 [6, 512, 4096], P('batch', 'lat', 'lon'), parts along dimension 0, may hold values from -6 to 6
- stem_weight: bfloat16 [4, 768, 1024], replicated, may hold values from -0.109375 to 0.109375
- down_weight: bfloat16 [1024, 512], replicated, may hold values from -0.1875 to 0.1875
- height_qkv: bfloat16 [512, 1024], replicated, may hold values from -0.25 to 0.25
- height_bias: float32 [8, 63], replicated, may hold values from -1.5 to 301.5
- width_qkv: bfloat16 [512, 1024], replicated, may hold values from -0.25 to 0.25
- width_bias: float32 [8, 256], replicated, may hold values from -1.5 to 301.5
- up_weight: bfloat16 [512, 1024], replicated, may hold values from -0.25 to 0.25
Outputs:
- block_output: bfloat16 [64, 256, 1024], P(('batch', 'lat'), 'lon'), parts along dimension 0
There are 2 independent parts, one for each index of `batch`. A program takes and returns all parts, laid end to end along the dimension named above; an argument that names none is the same for every part. Nothing has to cross between parts.
All inputs are finite; a program needn't handle non-finite values.
Results may differ from a plain program's by a relative error of at most 0.012.
Values may be sent and summed in bfloat16 or wider, within the bound.
A program may use at most 128 MiB of HBM per device.

v0:
```python
import jax
import jax.numpy as jnp
from jax import lax
from jax.sharding import PartitionSpec as P

QK = 256
VD = 512
HEADS = 8
PATCH = 16
DQ = 32
DV = 64


lowest_score = -1e30


def extended(cells, sides, width, closed):
    for axis, dim in sides:
        count = lax.axis_size(axis)
        ends = count if closed else count - 1
        head = lax.slice_in_dim(cells, 0, width, axis=dim)
        tail = lax.slice_in_dim(cells, cells.shape[dim] - width, cells.shape[dim], axis=dim)
        cells = jnp.concatenate(
            [
                lax.ppermute(tail, axis, [(i, (i + 1) % count) for i in range(ends)]),
                cells,
                lax.ppermute(head, axis, [((i + 1) % count, i) for i in range(ends)]),
            ],
            axis=dim,
        )
    return cells


def stem_features(padded, stem_weight, map_rows, map_cols):
    channels = padded.shape[0]
    blocks = padded.reshape(channels, map_rows + 1, PATCH, map_cols + 1, PATCH)
    blocks = blocks.transpose(1, 3, 0, 2, 4).reshape(
        map_rows + 1, map_cols + 1, channels * PATCH * PATCH
    )
    summed = jnp.zeros((map_rows * map_cols, stem_weight.shape[2]), jnp.float32)
    for row_shift in range(2):
        for col_shift in range(2):
            window = blocks[row_shift : row_shift + map_rows, col_shift : col_shift + map_cols]
            window = window.reshape(map_rows * map_cols, channels * PATCH * PATCH)
            summed = summed + jnp.dot(
                window, stem_weight[2 * row_shift + col_shift], preferred_element_type=jnp.float32
            )
    return jax.nn.relu(summed).astype(jnp.bfloat16)


def online_update(carried, scores, value_heads, form):
    running_max, denominator, weighted = carried
    new_peak = jnp.maximum(running_max, jnp.max(scores, axis=-1))
    weights = jnp.exp(scores - new_peak[..., None])
    denominator = jnp.sum(weights, axis=-1)
    weighted = jnp.einsum(
        form, weights.astype(jnp.bfloat16), value_heads, preferred_element_type=jnp.float32
    )
    return (new_peak, denominator, weighted)


def on_device(
    imagery, stem_weight, down_weight, height_qkv, height_bias, width_qkv, width_bias, up_weight
):
    rim_width = PATCH // 2
    widened = extended(imagery, (("lon", 2),), rim_width, True)
    padded = extended(widened, (("lat", 1),), rim_width, False)
    map_rows = imagery.shape[1] // PATCH
    map_cols = imagery.shape[2] // PATCH
    full_height = map_rows * lax.axis_size("lat")
    full_width = map_cols * lax.axis_size("lon")
    row_first = lax.axis_index("lat") * map_rows
    col_first = lax.axis_index("lon") * map_cols
    score_scale = DQ ** (-0.5)
    features = stem_features(padded, stem_weight, map_rows, map_cols)
    middle = jax.nn.relu(jnp.dot(features, down_weight, preferred_element_type=jnp.float32)).astype(
        jnp.bfloat16
    )
    height_proj = jnp.dot(middle, height_qkv, preferred_element_type=jnp.float32).astype(
        jnp.bfloat16
    )
    height_proj = height_proj.reshape(map_rows, map_cols, 2 * QK + VD)
    height_queries = height_proj[..., :QK].reshape(map_rows, map_cols, HEADS, DQ)
    initial = (
        jnp.full((HEADS, map_cols, map_rows), lowest_score, jnp.float32),
        jnp.zeros((HEADS, map_cols, map_rows), jnp.float32),
        jnp.zeros((HEADS, map_cols, map_rows, DV), jnp.float32),
    )
    key_rows = lax.all_gather(height_proj[..., QK : 2 * QK], "lat", axis=0, tiled=True)
    value_rows = lax.all_gather(height_proj[..., 2 * QK :], "lat", axis=0, tiled=True)
    key_count = key_rows.shape[0]
    scores = (
        jnp.einsum(
            "pwnd,ownd->nwpo",
            height_queries,
            key_rows.reshape(key_count, map_cols, HEADS, DQ),
            preferred_element_type=jnp.float32,
        )
        * score_scale
    )
    offsets = (
        jnp.arange(key_count, dtype=jnp.int32)[None, :]
        - (row_first + jnp.arange(map_rows, dtype=jnp.int32))[:, None]
        + full_height
        - 1
    )
    scores = scores + jnp.take(height_bias, offsets, axis=1)[:, None]
    running_max, denominator, weighted = online_update(
        initial, scores, value_rows.reshape(key_count, map_cols, HEADS, DV), "nwpo,ownd->nwpd"
    )
    height_out = (
        (weighted / denominator[..., None])
        .transpose(2, 1, 0, 3)
        .reshape(map_rows, map_cols, VD)
        .astype(jnp.bfloat16)
    )
    width_proj = jnp.dot(
        height_out.reshape(map_rows * map_cols, VD), width_qkv, preferred_element_type=jnp.float32
    ).astype(jnp.bfloat16)
    width_proj = width_proj.reshape(map_rows, map_cols, 2 * QK + VD)
    width_queries = width_proj[..., :QK].reshape(map_rows, map_cols, HEADS, DQ)
    width_initial = (
        jnp.full((HEADS, map_rows, map_cols), lowest_score, jnp.float32),
        jnp.zeros((HEADS, map_rows, map_cols), jnp.float32),
        jnp.zeros((HEADS, map_rows, map_cols, DV), jnp.float32),
    )
    key_cols = lax.all_gather(width_proj[..., QK : 2 * QK], "lon", axis=1, tiled=True)
    value_cols = lax.all_gather(width_proj[..., 2 * QK :], "lon", axis=1, tiled=True)
    key_count = key_cols.shape[1]
    scores = (
        jnp.einsum(
            "hwnd,hknd->nhwk",
            width_queries,
            key_cols.reshape(map_rows, key_count, HEADS, DQ),
            preferred_element_type=jnp.float32,
        )
        * score_scale
    )
    offsets = (
        jnp.arange(key_count, dtype=jnp.int32)[None, :]
        - (col_first + jnp.arange(map_cols, dtype=jnp.int32))[:, None]
    ) % full_width
    scores = scores + jnp.take(width_bias, offsets, axis=1)[:, None]
    width_max, width_denominator, width_weighted = online_update(
        width_initial, scores, value_cols.reshape(map_rows, key_count, HEADS, DV), "nhwk,hknd->nhwd"
    )
    width_out = (
        (width_weighted / width_denominator[..., None])
        .transpose(1, 2, 0, 3)
        .reshape(map_rows * map_cols, VD)
        .astype(jnp.bfloat16)
    )
    branch = jnp.dot(jax.nn.relu(width_out), up_weight, preferred_element_type=jnp.float32)
    result = jax.nn.relu(features.astype(jnp.float32) + branch).astype(jnp.bfloat16)
    return result.reshape(map_rows, map_cols, up_weight.shape[1])


def solution(mesh):
    placed = (P("batch", "lat", "lon"), P(), P(), P(), P(), P(), P(), P())
    return jax.shard_map(
        on_device,
        mesh=mesh,
        in_specs=placed,
        out_specs=P(("batch", "lat"), "lon", None),
        check_vma=False,
    )
```

profile of v0, /device:TPU:0, one launch (start us, length us, event | category | flops | bytes accessed | tf_op | source)
XLA Modules:
  0.0 249.6 jit_solution(9862370127342275498)
XLA Ops:
  7.7 3.0 %collective-permute-start = (bf16[3,128,8]{2,1,0:T(8,128)(2,1)S(1)}, bf16[3,128,8]{2,1,0:T(8,128)(2,1)S(1)}, u32[]{:S(2)}, u32[]{:S(2)}) collective-permute-start(bf16[3,128,8]{2,1,0:T(8,128)(2,1)S(1)} %get-tuple-element.16), channel_id=1, source_target_pairs={{0,4},{4,8},{8,12},{12,0},{1,5},{5,9},{9,13},{13,1},{2,6},{6,10},{... | collective-permute-start | bytes 18440 | tf_op jit(solution)/shard_map/ppermute | solution.py:25
  11.7 3.4 %collective-permute-done = bf16[3,128,8]{2,1,0:T(8,128)(2,1)S(1)} collective-permute-done((bf16[3,128,8]{2,1,0:T(8,128)(2,1)S(1)}, bf16[3,128,8]{2,1,0:T(8,128)(2,1)S(1)}, u32[]{:S(2)}, u32[]{:S(2)}) %collective-permute-start) | collective-permute-done | bytes 6176 | tf_op jit(solution)/shard_map/ppermute | solution.py:25
  18.6 3.5 %collective-permute-start.2 = (bf16[3,8,1040]{2,1,0:T(8,128)(2,1)S(1)}, bf16[3,8,1040]{2,1,0:T(8,128)(2,1)S(1)}, u32[]{:S(2)}, u32[]{:S(2)}) collective-permute-start(bf16[3,8,1040]{2,1,0:T(8,128)(2,1)S(1)} %get-tuple-element.13), channel_id=1, source_target_pairs={{0,1},{1,2},{2,3},{4,5},{5,6},{6,7},{8,9},{9,10},{10,11},{12,13},{... | collective-permute-start | bytes 149768 | tf_op jit(solution)/shard_map/ppermute | solution.py:25
  23.9 4.3 %collective-permute-done.3 = bf16[3,8,1040]{2,1,0:T(8,128)(2,1)S(1)} collective-permute-done((bf16[3,8,1040]{2,1,0:T(8,128)(2,1)S(1)}, bf16[3,8,1040]{2,1,0:T(8,128)(2,1)S(1)}, u32[]{:S(2)}, u32[]{:S(2)}) %collective-permute-start.3) | collective-permute-done | bytes 49952 | tf_op jit(solution)/shard_map/ppermute | solution.py:27
  28.3 6.8 %reshape.225 = bf16[3,9,16,65,16]{4,3,2,1,0:T(8,128)(2,1)} reshape(bf16[3,144,1040]{2,1,0:T(8,128)(2,1)S(1)} %pad_maximum_fusion) | data formatting | bytes 1797120 | tf_op jit(solution)/shard_map/reshape | solution.py:36
  35.0 7.2 %copy.53 = bf16[9,65,3,16,16]{1,4,3,2,0:T(8,128)(2,1)S(1)} copy(bf16[9,65,3,16,16]{4,1,3,0,2:T(8,128)(2,1)} %bitcast.68) | data formatting | bytes 1797120 | tf_op jit(solution)/shard_map/transpose | solution.py:37
  42.2 3.7 %fusion.58 = (bf16[8,64,768]{1,2,0:T(8,128)(2,1)}, bf16[8,64,768]{1,2,0:T(8,128)(2,1)}, bf16[8,64,768]{1,2,0:T(8,128)(2,1)}, bf16[8,64,768]{1,2,0:T(8,128)(2,1)}) fusion(bf16[9,65,768]{1,2,0:T(8,128)(2,1)S(1)} %bitcast.67), kind=kLoop, calls=%fused_computation.83 | loop fusion | bytes 6291456 | tf_op jit(solution)/shard_map/slice | solution.py:43
  49.1 3.8 %fusion.19 = f32[512,1024]{1,0:T(8,128)} fusion(bf16[512,768]{1,0:T(8,128)(2,1)S(1)} %bitcast.80, bf16[4,768,1024]{2,1,0:T(8,128)(2,1)} %param.9), kind=kOutput, calls=%fused_computation.26 | convolution fusion | flops 805306368 | bytes 4456448 | tf_op jit(solution)/shard_map/dot_general | solution.py:45
  52.9 3.8 %fusion.21 = f32[512,1024]{1,0:T(8,128)} fusion(bf16[512,768]{1,0:T(8,128)(2,1)S(1)} %bitcast.81, bf16[4,768,1024]{2,1,0:T(8,128)(2,1)} %param.9), kind=kOutput, calls=%fused_computation.28 | convolution fusion | flops 805306368 | bytes 4456448 | tf_op jit(solution)/shard_map/dot_general | solution.py:45
  57.4 3.9 %fusion.23 = f32[512,1024]{1,0:T(8,128)} fusion(bf16[512,768]{1,0:T(8,128)(2,1)S(1)} %bitcast.82, bf16[4,768,1024]{2,1,0:T(8,128)(2,1)} %param.9), kind=kOutput, calls=%fused_computation.30 | convolution fusion | flops 805306368 | bytes 4456448 | tf_op jit(solution)/shard_map/dot_general | solution.py:45
  61.9 4.4 %maximum_convert_fusion.1 = bf16[512,1024]{1,0:T(8,128)(2,1)S(1)} fusion(f32[512,1024]{1,0:T(8,128)} %fusion.19, f32[512,1024]{1,0:T(8,128)} %fusion.23, f32[512,1024]{1,0:T(8,128)} %fusion.21, bf16[512,768]{1,0:T(8,128)(2,1)S(1)} %bitcast.72, bf16[4,768,1024]{2,1,0:T(8,128)(2,1)} %param.9), kind=kOutput, calls=%fused_computation.21 | convolution fusion | flops 807927808 | bytes 9699328 | tf_op jit(solution)/shard_map/dot_general | solution.py:45
  66.3 2.9 %convolution_convert_fusion.1 = bf16[512,1024]{1,0:T(8,128)(2,1)S(1)} fusion(bf16[512,1024]{1,0:T(8,128)(2,1)S(1)} %copy-done, bf16[512,1024]{1,0:T(8,128)(2,1)S(1)} %maximum_convert_fusion.1, bf16[1024,512]{1,0:T(8,128)(2,1)} %param.10), kind=kOutput, calls=%fused_computation.37 | convolution fusion | flops 1074790400 | bytes 4194304 | tf_op jit(solution)/shard_map/dot_general | solution.py:79
  73.2 24.3 %all-gather.5.cloned.1.call-done = bf16[32,64,256]{2,1,0:T(8,128)(2,1)} async-done(((bf16[8,64,256]{2,1,0:T(8,128)(2,1)}), bf16[32,64,256]{2,1,0:T(8,128)(2,1)}) %all-gather.5.cloned.1.call-update) | async-done | bytes 1048592 | tf_op jit(solution)/shard_map/all_gather | solution.py:89
  97.5 2.0 copy.59
  99.5 6.5 %copy.61 = bf16[32,64,8,32]{3,0,1,2:T(8,128)(2,1)} copy(bf16[32,64,8,32]{1,3,2,0:T(8,128)(2,1)S(1)} %bitcast.70) | data formatting | bytes 2097152 | tf_op jit(solution)/shard_map/reshape | solution.py:96
  106.0 4.7 %fusion.13 = (f32[8,64,8]{2,1,0:T(8,128)S(1)}, f32[8,64,8,32]{3,2,1,0:T(8,128)S(1)}) fusion(f32[8,8,32]{2,1,0:T(8,128)S(1)} %select_bitcast_fusion.1, bf16[8,64,8,32]{3,0,1,2:T(8,128)(2,1)S(1)} %copy.60, bf16[32,64,8,32]{3,0,1,2:T(8,128)(2,1)} %copy.61), kind=kOutput, calls=%fused_computation.22 | convolution fusion | flops 8777728 | bytes 1859584 | tf_op jit(solution)/shard_map/pwnd,ownd->nwpo/dot_general | solution.py:93
  112.1 32.4 %all-gather.7.cloned.1.call-done = bf16[32,64,512]{2,1,0:T(8,128)(2,1)} async-done(((bf16[8,64,512]{2,1,0:T(8,128)(2,1)}), bf16[32,64,512]{2,1,0:T(8,128)(2,1)}) %all-gather.7.cloned.1.call-update) | async-done | bytes 2097168 | tf_op jit(solution)/shard_map/all_gather | solution.py:90
  144.5 6.2 %reshape.234 = bf16[32,64,8,64]{3,2,1,0:T(8,128)(2,1)} reshape(bf16[32,64,512]{2,1,0:T(8,128)(2,1)} %all-gather.7.cloned.1.call-done) | data formatting | bytes 4194304 | tf_op jit(solution)/shard_map/reshape | solution.py:109
  150.6 8.5 %fusion.8 = bf16[8,64,8,64]{3,0,1,2:T(8,128)(2,1)S(1)} fusion(bf16[32,64,8,64]{3,2,1,0:T(8,128)(2,1)} %reshape.234, f32[8,64,8,32]{3,2,1,0:T(8,128)S(1)} %get-tuple-element.18, f32[8,64,8]{0,1,2:T(8,128)S(1)} %bitcast.84, f32[8,64,8]{2,1,0:T(8,128)S(1)} %broadcast_maximum_fusion, f32[8,8,32]{2,1,0:T(8,128)S(1)} %select_bitcast_fusion.1), kind=kOutput, calls=%fused_computation.13 | convolution fusion | flops 17825792 | bytes 3186688 | tf_op jit(solution)/shard_map/nwpo,ownd->nwpd/dot_general | solution.py:56
  165.1 54.8 %gather_fusion.1 = f32[16384,8]{1,0:T(8,128)} fusion(f32[8,256]{0,1:T(8,128)S(1)} %copy.71, s32[16384]{0:T(1024)S(1)} %broadcast_clamp_fusion), kind=kCustom, calls=%fused_computation.1 | custom fusion | bytes 1114112 | tf_op jit(solution)/shard_map/jit(_take)/gather | solution.py:143
  219.9 5.2 %copy.72 = f32[64,256,8]{1,0,2:T(8,128)S(1)} copy(f32[64,256,8]{2,1,0:T(8,128)} %bitcast.69) | data formatting | bytes 1048576 | tf_op jit(solution)/shard_map/jit(_take)/gather | solution.py:143
  231.7 3.0 %copy.74 = bf16[8,256,512]{1,2,0:T(8,128)(2,1)S(1)} copy(bf16[8,256,512]{2,0,1:T(8,128)(2,1)} %all-gather.11.cloned.1.call-done) | data formatting | bytes 4194304 | tf_op jit(solution)/shard_map/all_gather | solution.py:128
  234.7 3.1 %fusion.36 = bf16[8,64,8,64]{3,1,0,2:T(8,128)(2,1)S(1)} fusion(f32[8,64,8]{1,0,2:T(8,128)S(1)} %bitcast.86, bf16[8,256,8,64]{1,3,2,0:T(8,128)(2,1)S(1)} %bitcast.75, f32[8,8,64,256]{3,2,1,0:T(8,128)} %copy-done.2, f32[8,8,64]{2,1,0:T(8,128)S(1)} %broadcast_maximum_fusion.1, f32[8,64,256]{2,1,0:T(8,128)S(1)} %select_bitcast_fusion), kind=kOutput, calls=%fused_computation.45 | convolution fusion | flops 139198464 | bytes 7372800 | tf_op jit(solution)/shard_map/nhwk,hknd->nhwd/dot_general | solution.py:56
  240.0 3.1 %maximum_convert_fusion = bf16[512,1024]{1,0:T(8,128)(2,1)} fusion(bf16[512,1024]{1,0:T(8,128)(2,1)S(1)} %copy-done.7, bf16[512,512]{1,0:T(8,128)(2,1)} %max.37, bf16[512,1024]{1,0:T(8,128)(2,1)} %param.15), kind=kOutput, calls=%fused_computation.15 | convolution fusion | flops 538968064 | bytes 3670016 | tf_op jit(solution)/shard_map/dot_general | solution.py:153
  (80 shorter events, 32.0 us)
Async XLA Ops:
  6.5 59.8 %copy-start = (bf16[512,1024]{1,0:T(8,128)(2,1)S(1)}, bf16[512,1024]{1,0:T(8,128)(2,1)}, u32[]{:S(2)}) copy-start(bf16[512,1024]{1,0:T(8,128)(2,1)} %param.11) | copy-start | bytes 3145732
  6.5 90.9 %all-gather.5.cloned.1.call-start = ((), (), s32[]{:S(2)}) async-start(), calls=%async_computation | async-start | bytes 1310720 | tf_op jit(solution)/shard_map/all_gather | solution.py:89
  7.7 7.4 %collective-permute-start = (bf16[3,128,8]{2,1,0:T(8,128)(2,1)S(1)}, bf16[3,128,8]{2,1,0:T(8,128)(2,1)S(1)}, u32[]{:S(2)}, u32[]{:S(2)}) collective-permute-start(bf16[3,128,8]{2,1,0:T(8,128)(2,1)S(1)} %get-tuple-element.16), channel_id=1, source_target_pairs={{0,4},{4,8},{8,12},{12,0},{1,5},{5,9},{9,13},{13,1},{2,6},{6,10},{... | collective-permute-start | bytes 18440 | tf_op jit(solution)/shard_map/ppermute | solution.py:25
  10.7 6.1 %collective-permute-start.1 = (bf16[3,128,8]{2,1,0:T(8,128)(2,1)S(1)}, bf16[3,128,8]{2,1,0:T(8,128)(2,1)S(1)}, u32[]{:S(2)}, u32[]{:S(2)}) collective-permute-start(bf16[3,128,8]{2,1,0:T(8,128)(2,1)S(1)} %get-tuple-element.15), channel_id=1, source_target_pairs={{4,0},{8,4},{12,8},{0,12},{5,1},{9,5},{13,9},{1,13},{6,2},{10,6},{... | collective-permute-start | bytes 18440 | tf_op jit(solution)/shard_map/ppermute | solution.py:27
  18.6 5.3 %collective-permute-start.2 = (bf16[3,8,1040]{2,1,0:T(8,128)(2,1)S(1)}, bf16[3,8,1040]{2,1,0:T(8,128)(2,1)S(1)}, u32[]{:S(2)}, u32[]{:S(2)}) collective-permute-start(bf16[3,8,1040]{2,1,0:T(8,128)(2,1)S(1)} %get-tuple-element.13), channel_id=1, source_target_pairs={{0,1},{1,2},{2,3},{4,5},{5,6},{6,7},{8,9},{9,10},{10,11},{12,13},{... | collective-permute-start | bytes 149768 | tf_op jit(solution)/shard_map/ppermute | solution.py:25
  22.1 6.0 %collective-permute-start.3 = (bf16[3,8,1040]{2,1,0:T(8,128)(2,1)S(1)}, bf16[3,8,1040]{2,1,0:T(8,128)(2,1)S(1)}, u32[]{:S(2)}, u32[]{:S(2)}) collective-permute-start(bf16[3,8,1040]{2,1,0:T(8,128)(2,1)S(1)} %get-tuple-element.14), channel_id=1, source_target_pairs={{1,0},{2,1},{3,2},{5,4},{6,5},{7,6},{9,8},{10,9},{11,10},{13,12},{... | collective-permute-start | bytes 149768 | tf_op jit(solution)/shard_map/ppermute | solution.py:27
  45.9 1.9 copy-start.5
  49.1 3.8 %copy-start.8 = (bf16[8,64,768]{2,1,0:T(8,128)(2,1)S(1)}, bf16[8,64,768]{2,1,0:T(8,128)(2,1)}, u32[]{:S(2)}) copy-start(bf16[8,64,768]{2,1,0:T(8,128)(2,1)} %copy.55) | copy-start | bytes 2359300
  52.9 3.8 %copy-start.4 = (bf16[8,64,768]{1,2,0:T(8,128)(2,1)S(1)}, bf16[8,64,768]{1,2,0:T(8,128)(2,1)}, u32[]{:S(2)}) copy-start(bf16[8,64,768]{1,2,0:T(8,128)(2,1)} %get-tuple-element.8) | copy-start | bytes 2359300
  57.4 3.9 %copy-start.3 = (bf16[8,64,768]{1,2,0:T(8,128)(2,1)S(1)}, bf16[8,64,768]{1,2,0:T(8,128)(2,1)}, u32[]{:S(2)}) copy-start(bf16[8,64,768]{1,2,0:T(8,128)(2,1)} %get-tuple-element.5) | copy-start | bytes 2359300
  66.3 2.9 %copy-start.6 = (bf16[512,1024]{1,0:T(8,128)(2,1)}, bf16[512,1024]{1,0:T(8,128)(2,1)S(1)}, u32[]{:S(2)}) copy-start(bf16[512,1024]{1,0:T(8,128)(2,1)S(1)} %maximum_convert_fusion.1) | copy-start | bytes 3145732
  69.2 2.1 copy-start.10
  70.0 74.5 %all-gather.7.cloned.1.call-start = ((), (), s32[]{:S(2)}) async-start(), calls=%async_computation.1 | async-start | bytes 2621440 | tf_op jit(solution)/shard_map/all_gather | solution.py:90
  70.9 154.6 %all-gather.9.cloned.1.call-start = ((), (), s32[]{:S(2)}) async-start(), calls=%async_computation.2 | async-start | bytes 1310720 | tf_op jit(solution)/shard_map/all_gather | solution.py:127
  162.4 2.6 %copy-start.9 = (f32[8,256]{1,0:T(8,128)S(1)}, f32[8,256]{1,0:T(8,128)}, u32[]{:S(2)}) copy-start(f32[8,256]{1,0:T(8,128)} %param.14) | copy-start | bytes 24580
  163.3 68.4 %all-gather.11.cloned.1.call-start = ((), (), s32[]{:S(2)}) async-start(), calls=%async_computation.3 | async-start | bytes 2621440 | tf_op jit(solution)/shard_map/all_gather | solution.py:128
  228.3 1.9 copy-start.2
  237.9 2.2 copy-start.7
  238.6 4.5 %copy-start.1 = (bf16[512,1024]{1,0:T(8,128)(2,1)S(1)}, bf16[512,1024]{1,0:T(8,128)(2,1)}, u32[]{:S(2)}) copy-start(bf16[512,1024]{1,0:T(8,128)(2,1)} %param.11) | copy-start | bytes 3145732
Sparse Core Ops, SparseCore 0:
  70.1 27.2 all-gather.4
  99.0 45.3 all-gather.6
  163.5 25.3 all-gather.8
  190.6 35.2 all-gather.10
where the time goes:
time: 250 us
  local copies, waits for them, and re-layouts  116 us (46%)
  waiting for transfers between devices  66.6 us (27%)
  matrix products  41.2 us (16%)
  between operations  13.5 us (5%)
  starting transfers between devices  9.32 us (4%)
  other arithmetic  3.35 us (1%)
    gather x2, local copies, waits for them, and re-layouts, on_device(): scores = scores + jnp.take(width_bias, offsets, axis=1)[:, None]  59.9 us
    all_gather x1, waiting for transfers between devices, on_device(): lax.all_gather(height_proj[..., 2 * QK:], 'lat', axis=0, tiled=True)  32.4 us
    all_gather x1, waiting for transfers between devices, on_device(): lax.all_gather(height_proj[..., QK:2 * QK], 'lat', axis=0, tiled=True)  24.3 us
    dot_general x4, matrix products, stem_features(): jnp.dot(window, stem_weight[2 * row_shift + col_shift], preferred_element...  15.8 us
    dot_general x2, matrix products, online_update(): jnp.einsum(form, weights.astype(jnp.bfloat16), value_heads, preferred_ele...  11.6 us
    slice x5, local copies, waits for them, and re-layouts, stem_features(): blocks[row_shift:row_shift + map_rows, col_shift:col_shift + map_cols]  8.17 us
    transpose x1, local copies, waits for them, and re-layouts, stem_features(): blocks.transpose(1, 3, 0, 2, 4)  7.16 us
    reshape x1, local copies, waits for them, and re-layouts, stem_features(): blocks = padded.reshape(channels, map_rows + 1, PATCH, map_cols + 1, PATCH)  6.77 us
  transfers between devices with their start and end apart: 8, of which 6 were waited for; matrix products, arithmetic and copies ran while one was open for 33% of the time, Pallas kernels for 0%

commit v1 on v0

--- a/solution.py
+++ b/solution.py
@@ -1,6 +1,10 @@
+import functools
+
 import jax
 import jax.numpy as jnp
 from jax import lax
+from jax.experimental import pallas as pl
+from jax.experimental.pallas import tpu as pltpu
 from jax.sharding import PartitionSpec as P
 
 QK = 256
@@ -155,10 +159,448 @@
     return result.reshape(map_rows, map_cols, up_weight.shape[1])
 
 
+MESH = pl.DeviceIdType.MESH
+ANY = pl.BlockSpec(memory_space=pl.ANY)
+VMEM = pl.BlockSpec(memory_space=pltpu.VMEM)
+BLOCK = 128
+VMEM_BYTES = 56 * 1024 * 1024
+
+
+def greet(lats, lons):
+    lat, lon = lax.axis_index("lat"), lax.axis_index("lon")
+    barrier = pltpu.get_barrier_semaphore()
+
+    def signal(step, carry):
+        there = lax.rem(lon * lats + lat + step, lats * lons)
+        pl.semaphore_signal(
+            barrier,
+            inc=1,
+            device_id={"lat": lax.rem(there, lats), "lon": there // lats},
+            device_id_type=MESH,
+        )
+        return carry
+
+    lax.fori_loop(1, lats * lons, signal, 0)
+    return barrier
+
+
+def chunks_turned(tile, to_bands, pick, to_rows):
+    turned = jnp.take_along_axis(tile, to_bands, axis=1, mode="promise_in_bounds")
+    turned = jnp.take_along_axis(turned, pick, axis=0, mode="promise_in_bounds")
+    return jnp.take_along_axis(turned, to_rows, axis=1, mode="promise_in_bounds")
+
+
+def stem_kernel(
+    lats, lons, img, stem_hbm, down_hbm, feat_ref, mid_ref,
+    ext, stem_w, down_w, xs, outbox, inbox,
+    load_sems, halo_send, halo_recv, send_sems, recv_sems,
+):
+    lat, lon = lax.axis_index("lat"), lax.axis_index("lon")
+    barrier = greet(lats, lons)
+    rows, cols = img.shape[1], img.shape[2]
+    local = pltpu.make_async_copy(
+        img, ext.at[:, pl.ds(16, rows), pl.ds(128, cols)], load_sems.at[0]
+    )
+    local.start()
+    load_stem = pltpu.make_async_copy(stem_hbm, stem_w, load_sems.at[1])
+    load_stem.start()
+    load_down = pltpu.make_async_copy(down_hbm, down_w, load_sems.at[2])
+    load_down.start()
+    west, east = lax.rem(lon + lons - 1, lons), lax.rem(lon + 1, lons)
+
+    @pl.when(lat == 0)
+    def _():
+        ext[:, 0:16, :] = jnp.zeros((3, 16, cols + 256), ext.dtype)
+
+    @pl.when(lat == lats - 1)
+    def _():
+        ext[:, rows + 16 : rows + 32, :] = jnp.zeros((3, 16, cols + 256), ext.dtype)
+
+    row_moves = {-1: (0, rows + 16, 16), 0: (0, 16, rows), 1: (rows - 16, 0, 16)}
+    col_moves = {-1: (0, cols + 128, 128), 0: (0, 128, cols), 1: (cols - 128, 0, 128)}
+    copies = []
+    for down in (0, -1, 1):
+        for right in (-1, 1, 0):
+            if down == 0 and right == 0:
+                continue
+            y_from, y_to, y_size = row_moves[down]
+            x_from, x_to, x_size = col_moves[right]
+            slot = len(copies)
+            copy = pltpu.make_async_remote_copy(
+                src_ref=img.at[:, pl.ds(y_from, y_size), pl.ds(x_from, x_size)],
+                dst_ref=ext.at[:, pl.ds(y_to, y_size), pl.ds(x_to, x_size)],
+                send_sem=halo_send.at[slot],
+                recv_sem=halo_recv.at[slot],
+                device_id={
+                    "lat": lax.rem(lat + down + lats, lats),
+                    "lon": {-1: west, 0: lon, 1: east}[right],
+                },
+                device_id_type=MESH,
+            )
+            copies.append((down, copy))
+    pl.semaphore_wait(barrier, lats * lons - 1)
+    for down, copy in copies:
+        if down == 0:
+            copy.start()
+        elif down == -1:
+            pl.when(lat > 0)(copy.start)
+        else:
+            pl.when(lat < lats - 1)(copy.start)
+    local.wait()
+    for down, copy in copies:
+        if down == 0:
+            copy.wait_send()
+            copy.wait_recv()
+        elif down == -1:
+            pl.when(lat > 0)(copy.wait_send)
+            pl.when(lat < lats - 1)(copy.wait_recv)
+        else:
+            pl.when(lat < lats - 1)(copy.wait_send)
+            pl.when(lat > 0)(copy.wait_recv)
+
+    lane = lax.broadcasted_iota(jnp.int32, (8, 128), 1)
+    sub = lax.broadcasted_iota(jnp.int32, (8, 128), 0)
+    to_bands = lax.rem(lane - 16 * sub + 128, 128)
+    pick = lax.rem(lane // 16 - sub + 8, 8)
+    to_rows = lax.rem(lane + 16 * sub, 128)
+    map_rows = rows // PATCH
+    tiles = cols // 128 + 1
+
+    def patch(i, carry):
+        for c in range(3):
+            slab = ext[c, pl.ds(pl.multiple_of(16 * i, 16), 32), :].astype(jnp.float32)
+            for half in range(2):
+                part = slab[8 + 8 * half : 16 + 8 * half, 120 : 120 + 128 * tiles]
+                for t in range(tiles):
+                    xs[i, 8 * t : 8 * t + 8, (2 * c + half) * 128 : (2 * c + half + 1) * 128] = (
+                        chunks_turned(part[:, 128 * t : 128 * t + 128], to_bands, pick, to_rows)
+                    )
+        return carry
+
+    lax.fori_loop(0, map_rows + 1, patch, 0)
+    load_stem.wait()
+    load_down.wait()
+    width = cols // PATCH // lats
+    depth = 3 * PATCH * PATCH
+
+    def sending(dest, k):
+        return pltpu.make_async_remote_copy(
+            src_ref=outbox.at[dest],
+            dst_ref=inbox.at[lat],
+            send_sem=send_sems.at[k],
+            recv_sem=recv_sems.at[k],
+            device_id={"lat": dest, "lon": lon},
+            device_id_type=MESH,
+        )
+
+    def group(k, carry):
+        dest = lax.rem(lat + k, lats)
+        first = pl.multiple_of(dest * width, width)
+        here = xs[:, pl.ds(first, width + 8), :]
+        x0 = here[:, :width, :].reshape((map_rows + 1) * width, depth).astype(jnp.bfloat16)
+        x1 = here[:, 1 : width + 1, :].reshape((map_rows + 1) * width, depth).astype(jnp.bfloat16)
+        count = map_rows * width
+        total = jnp.dot(x0[:count], stem_w[0], preferred_element_type=jnp.float32)
+        total += jnp.dot(x1[:count], stem_w[1], preferred_element_type=jnp.float32)
+        total += jnp.dot(x0[width:], stem_w[2], preferred_element_type=jnp.float32)
+        total += jnp.dot(x1[width:], stem_w[3], preferred_element_type=jnp.float32)
+        feats = jnp.maximum(total, 0.0).astype(jnp.bfloat16)
+        feat_ref[dest] = feats
+        middle = jnp.dot(feats, down_w[...], preferred_element_type=jnp.float32)
+        middle = jnp.maximum(middle, 0.0).astype(jnp.bfloat16)
+
+        @pl.when(k < lats)
+        def _():
+            outbox[dest] = middle
+            sending(dest, k).start()
+
+        @pl.when(k == lats)
+        def _():
+            inbox[lat] = middle
+
+        return carry
+
+    lax.fori_loop(1, lats + 1, group, 0)
+
+    def finish(k, carry):
+        sending(lax.rem(lat + k, lats), k).wait()
+        return carry
+
+    lax.fori_loop(1, lats, finish, 0)
+    mid_ref[...] = inbox[...]
+
+
+def softmaxed(q, k, v, bias):
+    count = q.shape[0]
+    lane = lax.broadcasted_iota(jnp.int32, (count, QK), 1) // DQ
+    pair_lane = lax.broadcasted_iota(jnp.int32, (count, 2 * DV), 1) // DV
+    outs = []
+    for pair in range(HEADS // 2):
+        halves = []
+        for n in (2 * pair, 2 * pair + 1):
+            q_head = jnp.where(lane == n, q, jnp.zeros_like(q))
+            scores = lax.dot_general(
+                q_head, k, (((1,), (1,)), ((), ())), preferred_element_type=jnp.float32
+            )
+            scores = scores * (DQ ** (-0.5)) + bias[n]
+            weights = jnp.exp(scores - jnp.max(scores, axis=-1, keepdims=True))
+            denominator = jnp.sum(weights, axis=-1, keepdims=True)
+            weighted = jnp.dot(
+                weights.astype(jnp.bfloat16),
+                v[:, 2 * DV * pair : 2 * DV * (pair + 1)],
+                preferred_element_type=jnp.float32,
+            )
+            halves.append(weighted / denominator)
+        outs.append(jnp.where(pair_lane == 0, halves[0], halves[1]))
+    return jnp.concatenate(outs, axis=1)
+
+
+def height_kernel(
+    lats, lons, mid_ref, qkv_ref, bias_ref, row_ref,
+    bias, proj, result, outbox, inbox, send_sems, recv_sems,
+):
+    lat, lon = lax.axis_index("lat"), lax.axis_index("lon")
+    barrier = greet(lats, lons)
+    positions = mid_ref.shape[0] * mid_ref.shape[1]
+    width = inbox.shape[1] // (lats * lons)
+    height = positions // width
+    own_rows = inbox.shape[0]
+    beside = BLOCK // height
+    i = lax.broadcasted_iota(jnp.int32, (BLOCK, BLOCK), 0)
+    j = lax.broadcasted_iota(jnp.int32, (BLOCK, BLOCK), 1)
+    for n in range(HEADS):
+        spread = jnp.broadcast_to(bias_ref[n : n + 1, :], (BLOCK, BLOCK))
+        turned = pltpu.roll(spread, BLOCK - (height - 1), 1, stride=1, stride_axis=0)
+        bias[n] = jnp.where(i // height == j // height, turned, lowest_score)
+    projected = jnp.dot(
+        mid_ref[...].reshape(positions, VD), qkv_ref[...], preferred_element_type=jnp.float32
+    )
+    for c in range(proj.shape[0]):
+        proj[c] = projected[:, 128 * c : 128 * c + 128]
+
+    def block(g, carry):
+        parts = [
+            jnp.concatenate(
+                [
+                    proj[c, pl.ds(g * beside + w, height, stride=width), :]
+                    for c in range(proj.shape[0])
+                ],
+                axis=1,
+            )
+            for w in range(beside)
+        ]
+        mine = jnp.concatenate(parts, axis=0).astype(jnp.bfloat16)
+        out = softmaxed(mine[:, :QK], mine[:, QK : 2 * QK], mine[:, 2 * QK :], bias)
+        for w in range(beside):
+            for c in range(result.shape[0]):
+                result[c, pl.ds(g * beside + w, height, stride=width), :] = out[
+                    w * height : (w + 1) * height, 128 * c : 128 * c + 128
+                ]
+        return carry
+
+    lax.fori_loop(0, width // beside, block, 0)
+    for c in range(result.shape[0]):
+        outbox[:, :, :, 128 * c : 128 * c + 128] = (
+            result[c].astype(jnp.bfloat16).reshape(outbox.shape[:3] + (128,))
+        )
+    pl.semaphore_wait(barrier, lats * lons - 1)
+    me = lat * lons + lon
+    others = lats * lons
+    column = pl.multiple_of((lon * lats + lat) * width, width)
+
+    def sending(k):
+        there = lax.rem(me + k, others)
+        return pltpu.make_async_remote_copy(
+            src_ref=outbox.at[there],
+            dst_ref=inbox.at[:, pl.ds(column, width), :],
+            send_sem=send_sems.at[k],
+            recv_sem=recv_sems.at[k],
+            device_id={"lat": there // lons, "lon": lax.rem(there, lons)},
+            device_id_type=MESH,
+        )
+
+    def start(k, carry):
+        sending(k).start()
+        return carry
+
+    lax.fori_loop(1, others, start, 0)
+    inbox[:, pl.ds(column, width), :] = outbox[me]
+
+    def finish(k, carry):
+        sending(k).wait()
+        return carry
+
+    lax.fori_loop(1, others, finish, 0)
+    row_ref[...] = inbox[...]
+
+
+def width_kernel(
+    lats, lons, row_ref, qkv_ref, bias_ref, wide_ref,
+    bias, outbox, inbox, send_sems, recv_sems,
+):
+    lon = lax.axis_index("lon")
+    barrier = pltpu.get_barrier_semaphore()
+    for k in range(1, lons):
+        pl.semaphore_signal(
+            barrier, inc=1, device_id={"lon": lax.rem(lon + k, lons)}, device_id_type=MESH
+        )
+    own_rows, full, _ = row_ref.shape
+    for n in range(HEADS):
+        spread = jnp.broadcast_to(bias_ref[n : n + 1, :], (full, full))
+        bias[n] = pltpu.roll(spread, 0, 1, stride=1, stride_axis=0)
+    part = full // lons
+
+    def row(r, carry):
+        mine = jnp.dot(row_ref[r], qkv_ref[...], preferred_element_type=jnp.float32).astype(
+            jnp.bfloat16
+        )
+        out = softmaxed(mine[:, :QK], mine[:, QK : 2 * QK], mine[:, 2 * QK :], bias)
+        out = jnp.maximum(out, 0.0).astype(jnp.bfloat16)
+        for d in range(lons):
+            outbox[d, r] = out[part * d : part * (d + 1)]
+        return carry
+
+    lax.fori_loop(0, own_rows, row, 0)
+    pl.semaphore_wait(barrier, lons - 1)
+
+    def sending(k):
+        there = lax.rem(lon + k, lons)
+        return pltpu.make_async_remote_copy(
+            src_ref=outbox.at[there],
+            dst_ref=inbox.at[lon],
+            send_sem=send_sems.at[k],
+            recv_sem=recv_sems.at[k],
+            device_id={"lon": there},
+            device_id_type=MESH,
+        )
+
+    for k in range(1, lons):
+        sending(k).start()
+    inbox[lon] = outbox[lon]
+    for k in range(1, lons):
+        sending(k).wait()
+    wide_ref[...] = inbox[...]
+
+
+def up_kernel(lats, wide_ref, feat_ref, up_ref, out_ref):
+    map_rows, map_cols, channels = out_ref.shape
+    width = map_cols // lats
+    for k in range(lats):
+        x = wide_ref[:, k * width : (k + 1) * width, :].reshape(map_rows * width, VD)
+        branch = jnp.dot(x, up_ref[...], preferred_element_type=jnp.float32)
+        total = jnp.maximum(feat_ref[k].astype(jnp.float32) + branch, 0.0)
+        out_ref[:, k * width : (k + 1) * width, :] = total.astype(jnp.bfloat16).reshape(
+            map_rows, width, channels
+        )
+
+
+def with_kernels(
+    imagery, stem_weight, down_weight, height_qkv, height_bias, width_qkv, width_bias, up_weight
+):
+    lats, lons = lax.axis_size("lat"), lax.axis_size("lon")
+    bf16, f32 = jnp.bfloat16, jnp.float32
+    _, rows, cols = imagery.shape
+    map_rows, map_cols = rows // PATCH, cols // PATCH
+    positions = map_rows * map_cols
+    channels = stem_weight.shape[2]
+    full_height, full_width = map_rows * lats, map_cols * lons
+    depth = stem_weight.shape[1]
+    width = map_cols // lats
+    own_rows = map_rows // lons
+    dma = pltpu.SemaphoreType.DMA
+
+    def params(number):
+        return pltpu.CompilerParams(
+            collective_id=number, has_side_effects=True, vmem_limit_bytes=VMEM_BYTES
+        )
+
+    feats, mid = pl.pallas_call(
+        functools.partial(stem_kernel, lats, lons),
+        name="stem",
+        out_shape=(
+            jax.ShapeDtypeStruct((lats, positions // lats, channels), bf16),
+            jax.ShapeDtypeStruct((lats, positions // lats, VD), bf16),
+        ),
+        in_specs=[ANY] * 3,
+        out_specs=(VMEM, VMEM),
+        scratch_shapes=[
+            pltpu.VMEM((3, rows + 32, cols + 256), bf16),
+            pltpu.VMEM(stem_weight.shape, bf16),
+            pltpu.VMEM(down_weight.shape, bf16),
+            pltpu.VMEM((map_rows + 1, map_cols + 8, depth), f32),
+            pltpu.VMEM((lats, positions // lats, VD), bf16),
+            pltpu.VMEM((lats, positions // lats, VD), bf16),
+            dma((3,)),
+            dma((8,)),
+            dma((8,)),
+            dma((lats,)),
+            dma((lats,)),
+        ],
+        compiler_params=params(0),
+    )(imagery, stem_weight, down_weight)
+    spread_bias = jnp.pad(height_bias, ((0, 0), (0, BLOCK - height_bias.shape[1])))
+    row = pl.pallas_call(
+        functools.partial(height_kernel, lats, lons),
+        name="height",
+        out_shape=jax.ShapeDtypeStruct((own_rows, full_width, VD), bf16),
+        in_specs=[VMEM] * 3,
+        out_specs=VMEM,
+        scratch_shapes=[
+            pltpu.VMEM((HEADS, BLOCK, BLOCK), f32),
+            pltpu.VMEM(((2 * QK + VD) // 128, positions, 128), f32),
+            pltpu.VMEM((VD // 128, positions, 128), f32),
+            pltpu.VMEM((lats * lons, own_rows, width, VD), bf16),
+            pltpu.VMEM((own_rows, full_width, VD), bf16),
+            dma((lats * lons,)),
+            dma((lats * lons,)),
+        ],
+        compiler_params=params(1),
+    )(mid, height_qkv, spread_bias)
+    wide = pl.pallas_call(
+        functools.partial(width_kernel, lats, lons),
+        name="width",
+        out_shape=jax.ShapeDtypeStruct((lons, own_rows, map_cols, VD), bf16),
+        in_specs=[VMEM] * 3,
+        out_specs=VMEM,
+        scratch_shapes=[
+            pltpu.VMEM((HEADS, full_width, full_width), f32),
+            pltpu.VMEM((lons, own_rows, map_cols, VD), bf16),
+            pltpu.VMEM((lons, own_rows, map_cols, VD), bf16),
+            dma((lons,)),
+            dma((lons,)),
+        ],
+        compiler_params=params(2),
+    )(row, width_qkv, width_bias)
+    return pl.pallas_call(
+        functools.partial(up_kernel, lats),
+        name="up",
+        out_shape=jax.ShapeDtypeStruct((map_rows, map_cols, channels), bf16),
+        in_specs=[VMEM] * 3,
+        out_specs=VMEM,
+        compiler_params=pltpu.CompilerParams(vmem_limit_bytes=VMEM_BYTES),
+    )(wide.reshape(map_rows, map_cols, VD), feats, up_weight)
+
+
+def either(*args):
+    lats, lons = lax.axis_size("lat"), lax.axis_size("lon")
+    _, rows, cols = args[0].shape
+    map_rows, map_cols = rows // PATCH, cols // PATCH
+    whole_tiles = (
+        map_cols % (16 * lats) == 0
+        and map_rows % lons == 0
+        and BLOCK % (map_rows * lats) == 0
+        and 2 * map_rows * lats - 1 <= BLOCK
+        and (map_cols // lats) % (BLOCK // (map_rows * lats)) == 0
+        and cols % 128 == 0
+        and map_rows % 8 == 0
+    )
+    return with_kernels(*args) if whole_tiles else on_device(*args)
+
+
 def solution(mesh):
     placed = (P("batch", "lat", "lon"), P(), P(), P(), P(), P(), P(), P())
     return jax.shard_map(
-        on_device,
+        either,
         mesh=mesh,
         in_specs=placed,
         out_specs=P(("batch", "lat"), "lon", None),

time: 250 us -> 66.5 us (0.27)
  local copies, waits for them, and re-layouts: 116 us -> 1.28 us
  waiting for transfers between devices: 66.6 us -> 0 us
  Pallas kernels: 0 us -> 64.1 us
  matrix products: 41.2 us -> 0 us
  between operations: 13.5 us -> 0.03 us
  starting transfers between devices: 9.32 us -> 0 us
  other arithmetic: 3.35 us -> 0 us
    pallas_call x0 -> x4, Pallas kernels: none -> 64.1 us  [the longest x1 27.7 us: with_kernels(): pl.pallas_call(functools.partial(stem_kernel, lats, lons), name='stem', o...]
    gather x4 -> x0, local copies, waits for them, and re-layouts: 60.7 us -> none  [the longest x2 59.9 us: on_device(): scores = scores + jnp.take(width_bias, offsets, axis=1)[:, None]]
    all_gather x4 -> x0, waiting for transfers between devices: 56.7 us -> none  [the longest x1 32.4 us: on_device(): lax.all_gather(height_proj[..., 2 * QK:], 'lat', axis=0, tiled=True)]
    dot_general x11 -> x0, matrix products: 41.2 us -> none  [the longest x4 15.8 us: stem_features(): jnp.dot(window, stem_weight[2 * row_shift + col_shift], preferred_element...]
    reshape x4 -> x0, local copies, waits for them, and re-layouts: 20 us -> none  [the longest x1 6.77 us: stem_features(): blocks = padded.reshape(channels, map_rows + 1, PATCH, map_cols + 1, PATCH)]
    slice x11 -> x0, local copies, waits for them, and re-layouts: 11 us -> none  [the longest x5 8.17 us: stem_features(): blocks[row_shift:row_shift + map_rows, col_shift:col_shift + map_cols]]
    ppermute x4 -> x0, waiting for transfers between devices: 9.83 us -> none  [the longest x2 5.92 us: extended(): lax.ppermute(head, axis, [((i + 1) % count, i) for i in range(ends)])]
    ppermute x4 -> x0, starting transfers between devices: 8.79 us -> none  [the longest x2 6.47 us: extended(): lax.ppermute(tail, axis, [(i, (i + 1) % count) for i in range(ends)])]
  transfers between devices with their start and end apart: 8 -> 0, of which waited for: 6 -> 0; matrix products, arithmetic and copies ran while one was open for 33% -> 0% of each run, Pallas kernels for 0% -> 0%
where the time goes in v1:
time: 66.5 us; the launch traced here: 65.4 us
  Pallas kernels  64.1 us (96%)
  local copies, waits for them, and re-layouts  1.28 us (2%)
    pallas_call x1, Pallas kernels, with_kernels(): pl.pallas_call(functools.partial(stem_kernel, lats, lons), name='stem', o...  27.7 us
    pallas_call x1, Pallas kernels, with_kernels(): pl.pallas_call(functools.partial(height_kernel, lats, lons), name='height...  19.4 us
    pallas_call x1, Pallas kernels, with_kernels(): pl.pallas_call(functools.partial(width_kernel, lats, lons), name='width',...  13.6 us
    pallas_call x1, Pallas kernels, with_kernels(): pl.pallas_call(functools.partial(up_kernel, lats), name='up', out_shape=j...  3.4 us

profile of v1, /device:TPU:0, one launch (start us, length us, event | category | flops | bytes accessed | tf_op | source)
XLA Modules:
  0.0 65.4 jit_solution(255620119186676097)
XLA Ops:
  0.0 1.3 %pad.4.bias_ref = f32[8,128]{1,0:T(8,128)} pad(f32[8,63]{1,0:T(8,128)} %param.12, f32[]{:T(128)} %constant.2.clone.1), padding=0_0x0_65 | pad | bytes 6116 | tf_op jit(solution)/shard_map/jit(_pad)/pad | solution.py:541
  1.3 27.7 %stem.1 = (bf16[4,128,1024]{2,1,0:T(8,128)(2,1)}, bf16[4,128,512]{2,1,0:T(8,128)(2,1)}) custom-call(bf16[3,128,1024]{2,1,0:T(8,128)(2,1)} %img.1, bf16[4,768,1024]{2,1,0:T(8,128)(2,1)} %stem_hbm.1, bf16[1024,512]{1,0:T(8,128)(2,1)} %down_hbm.1), custom_call_target="tpu_custom_call" | custom-call | tf_op jit(solution)/shard_map/stem/pallas_call | solution.py:517
  29.0 19.4 %height.1.row_ref = bf16[2,256,512]{2,1,0:T(8,128)(2,1)} custom-call(bf16[4,128,512]{2,1,0:T(8,128)(2,1)} %get-tuple-element.7.mid_ref, bf16[512,1024]{1,0:T(8,128)(2,1)} %qkv_ref.2, f32[8,128]{1,0:T(8,128)} %pad.4.bias_ref), custom_call_target="tpu_custom_call" | custom-call | tf_op jit(solution)/shard_map/height/pallas_call | solution.py:542
  48.4 13.6 %width.1 = bf16[4,2,64,512]{3,2,1,0:T(8,128)(2,1)} custom-call(bf16[2,256,512]{2,1,0:T(8,128)(2,1)} %height.1.row_ref, bf16[512,1024]{1,0:T(8,128)(2,1)} %qkv_ref.3, f32[8,256]{1,0:T(8,128)} %bias_ref.1), custom_call_target="tpu_custom_call" | custom-call | tf_op jit(solution)/shard_map/width/pallas_call | solution.py:559
  62.0 3.4 %up.1 = bf16[8,64,1024]{2,1,0:T(8,128)(2,1)} custom-call(bf16[8,64,512]{2,1,0:T(8,128)(2,1)} %bitcast.1, bf16[4,128,1024]{2,1,0:T(8,128)(2,1)} %get-tuple-element.8.feat_ref, bf16[512,1024]{1,0:T(8,128)(2,1)} %up_ref.1), custom_call_target="tpu_custom_call" | custom-call | tf_op jit(solution)/shard_map/up/pallas_call | solution.py:574

commit v2 on v0

--- a/solution.py
+++ b/solution.py
@@ -1,6 +1,10 @@
+import functools
+
 import jax
 import jax.numpy as jnp
 from jax import lax
+from jax.experimental import pallas as pl
+from jax.experimental.pallas import tpu as pltpu
 from jax.sharding import PartitionSpec as P
 
 QK = 256
@@ -155,10 +159,476 @@
     return result.reshape(map_rows, map_cols, up_weight.shape[1])
 
 
+MESH = pl.DeviceIdType.MESH
+ANY = pl.BlockSpec(memory_space=pl.ANY)
+VMEM = pl.BlockSpec(memory_space=pltpu.VMEM)
+BLOCK = 128
+HALVES = 2
+VMEM_BYTES = 58 * 1024 * 1024
+LOG2E = 1.4426950408889634
+
+
+def chunks_turned(tile, to_bands, pick, to_rows):
+    turned = jnp.take_along_axis(tile, to_bands, axis=1, mode="promise_in_bounds")
+    turned = jnp.take_along_axis(turned, pick, axis=0, mode="promise_in_bounds")
+    return jnp.take_along_axis(turned, to_rows, axis=1, mode="promise_in_bounds")
+
+
+def attention(q, k, v, bias):
+    count = q.shape[0]
+    lane = lax.broadcasted_iota(jnp.int32, (count, QK), 1) // DQ
+    first = lax.broadcasted_iota(jnp.int32, (count, 2 * DV), 1) < DV
+    outs = []
+    for pair in range(HEADS // 2):
+        values = v[:, 2 * DV * pair : 2 * DV * (pair + 1)]
+        ones = jnp.ones_like(values)
+        both = []
+        for n in (2 * pair, 2 * pair + 1):
+            q_head = jnp.where(lane == n, q, jnp.zeros_like(q))
+            scores = lax.dot_general(
+                q_head, k, (((1,), (1,)), ((), ())), preferred_element_type=jnp.float32
+            )
+            scores = scores * (DQ ** (-0.5) * LOG2E) + bias[n]
+            weights = jnp.exp2(scores - jnp.max(scores, axis=-1, keepdims=True))
+            held = jnp.where(first, values, ones) if n % 2 == 0 else jnp.where(first, ones, values)
+            both.append(
+                jnp.dot(weights.astype(jnp.bfloat16), held, preferred_element_type=jnp.float32)
+            )
+        totals = pltpu.roll(jnp.where(first, both[1], both[0]), DV, 1)
+        outs.append(jnp.where(first, both[0], both[1]) / totals)
+    return jnp.concatenate(outs, axis=1)
+
+
+def block_kernel(
+    lats, lons, img, stem_hbm, down_hbm, height_hbm, width_hbm, up_hbm, height_bias, width_bias,
+    out_ref,
+    ext, stem_w, down_w, height_w, width_w, up_w, xs, feats, padded_bias, bias_h, bias_w,
+    proj_h, result, proj_w, out_a, in_a, out_b, in_b, out_c, in_c,
+    load_sems, halo_send, halo_recv, send_a, recv_a, send_b, recv_b, send_c, recv_c,
+):
+    lat, lon = lax.axis_index("lat"), lax.axis_index("lon")
+    rows, cols = img.shape[1], img.shape[2]
+    map_rows, map_cols = rows // PATCH, cols // PATCH
+    full_height, full_width = map_rows * lats, map_cols * lons
+    width = map_cols // lats
+    own_rows = map_rows // lons
+    depth = 3 * PATCH * PATCH
+    others = lats * lons
+
+    barrier = pltpu.get_barrier_semaphore()
+
+    def greet(step, carry):
+        there = lax.rem(lon * lats + lat + step, others)
+        pl.semaphore_signal(
+            barrier,
+            inc=1,
+            device_id={"lat": lax.rem(there, lats), "lon": there // lats},
+            device_id_type=MESH,
+        )
+        return carry
+
+    lax.fori_loop(1, others, greet, 0)
+    local = pltpu.make_async_copy(
+        img, ext.at[:, pl.ds(16, rows), pl.ds(128, cols)], load_sems.at[0]
+    )
+    local.start()
+    loads = []
+    for number, (source, held) in enumerate(
+        (
+            (stem_hbm, stem_w),
+            (down_hbm, down_w),
+            (height_hbm, height_w),
+            (width_hbm, width_w),
+            (up_hbm, up_w),
+        )
+    ):
+        loads.append(pltpu.make_async_copy(source, held, load_sems.at[number + 1]))
+        loads[-1].start()
+    west, east = lax.rem(lon + lons - 1, lons), lax.rem(lon + 1, lons)
+
+    @pl.when(lat == 0)
+    def _():
+        ext[:, 0:16, :] = jnp.zeros((3, 16, cols + 256), ext.dtype)
+
+    @pl.when(lat == lats - 1)
+    def _():
+        ext[:, rows + 16 : rows + 32, :] = jnp.zeros((3, 16, cols + 256), ext.dtype)
+
+    row_moves = {-1: (0, rows + 16, 16), 0: (0, 16, rows), 1: (rows - 16, 0, 16)}
+    col_moves = {-1: (0, cols + 128, 128), 0: (0, 128, cols), 1: (cols - 128, 0, 128)}
+    copies = []
+    for down, right in ((-1, 0), (1, 0), (0, -1), (0, 1), (-1, -1), (-1, 1), (1, -1), (1, 1)):
+        y_from, y_to, y_size = row_moves[down]
+        x_from, x_to, x_size = col_moves[right]
+        slot = len(copies)
+        copy = pltpu.make_async_remote_copy(
+            src_ref=img.at[:, pl.ds(y_from, y_size), pl.ds(x_from, x_size)],
+            dst_ref=ext.at[:, pl.ds(y_to, y_size), pl.ds(x_to, x_size)],
+            send_sem=halo_send.at[slot],
+            recv_sem=halo_recv.at[slot],
+            device_id={
+                "lat": lax.rem(lat + down + lats, lats),
+                "lon": {-1: west, 0: lon, 1: east}[right],
+            },
+            device_id_type=MESH,
+        )
+        copies.append((down, copy))
+    pl.semaphore_wait(barrier, others - 1)
+    for down, copy in copies:
+        if down == 0:
+            copy.start()
+        elif down == -1:
+            pl.when(lat > 0)(copy.start)
+        else:
+            pl.when(lat < lats - 1)(copy.start)
+
+    lane = lax.broadcasted_iota(jnp.int32, (8, 128), 1)
+    sub = lax.broadcasted_iota(jnp.int32, (8, 128), 0)
+    to_bands = lax.rem(lane - 16 * sub + 128, 128)
+    pick = lax.rem(lane // 16 - sub + 8, 8)
+    to_rows = lax.rem(lane + 16 * sub, 128)
+    tiles = cols // 128 + 1
+
+    def patch(i, first, count):
+        for c in range(3):
+            slab = ext[
+                c,
+                pl.ds(pl.multiple_of(16 * i, 16), 32),
+                128 * first : 128 * (first + count + 1),
+            ].astype(jnp.float32)
+            for half in range(2):
+                part = slab[8 + 8 * half : 16 + 8 * half, 120 : 120 + 128 * count]
+                for t in range(count):
+                    at = 8 * (first + t)
+                    xs[i, at : at + 8, (2 * c + half) * 128 : (2 * c + half + 1) * 128] = (
+                        chunks_turned(part[:, 128 * t : 128 * t + 128], to_bands, pick, to_rows)
+                    )
+
+    def inner(i, carry):
+        patch(i, 1, tiles - 2)
+        return carry
+
+    def rim(i, carry):
+        patch(i, 0, 1)
+        patch(i, tiles - 1, 1)
+        return carry
+
+    local.wait()
+    lax.fori_loop(1, map_rows, inner, 0)
+
+    padded_bias[...] = jnp.zeros(padded_bias.shape, jnp.float32)
+    padded_bias[:, 0 : height_bias.shape[1]] = height_bias[...]
+    down_row = lax.broadcasted_iota(jnp.int32, (BLOCK, BLOCK), 0) // full_height
+    key_row = lax.broadcasted_iota(jnp.int32, (BLOCK, BLOCK), 1) // full_height
+    for n in range(HEADS):
+        spread = jnp.broadcast_to(padded_bias[n : n + 1, :] * LOG2E, (BLOCK, BLOCK))
+        turned = pltpu.roll(spread, BLOCK - (full_height - 1), 1, stride=1, stride_axis=0)
+        bias_h[n] = jnp.where(down_row == key_row, turned, lowest_score)
+        spread = jnp.broadcast_to(width_bias[n : n + 1, :] * LOG2E, (full_width, full_width))
+        bias_w[n] = pltpu.roll(spread, 0, 1, stride=1, stride_axis=0)
+
+    for down, copy in copies:
+        if down == 0:
+            copy.wait_send()
+            copy.wait_recv()
+        elif down == -1:
+            pl.when(lat > 0)(copy.wait_send)
+            pl.when(lat < lats - 1)(copy.wait_recv)
+        else:
+            pl.when(lat < lats - 1)(copy.wait_send)
+            pl.when(lat > 0)(copy.wait_recv)
+    patch(0, 1, tiles - 2)
+    patch(map_rows, 1, tiles - 2)
+    lax.fori_loop(0, map_rows + 1, rim, 0)
+
+    loads[0].wait()
+    loads[1].wait()
+
+    def far_first(step):
+        return jnp.where(step < lats // 2, lats // 2 + step, lats - 1 - step)
+
+    def partner(k):
+        other = lat
+        bit = 1
+        while bit < lats:
+            mine = lax.rem(lat // bit, 2)
+            flip = lax.rem(k // bit, 2)
+            other = other + bit * flip * (1 - 2 * mine)
+            bit *= 2
+        return other
+
+    def sending_a(k):
+        dest = partner(k)
+        return pltpu.make_async_remote_copy(
+            src_ref=out_a.at[dest],
+            dst_ref=in_a.at[lat],
+            send_sem=send_a.at[k],
+            recv_sem=recv_a.at[k],
+            device_id={"lat": dest, "lon": lon},
+            device_id_type=MESH,
+        )
+
+    def stem(step, carry):
+        k = far_first(step)
+        dest = partner(k)
+        first = pl.multiple_of(dest * width, width)
+        here = xs[:, pl.ds(first, width + 8), :]
+        x0 = here[:, :width, :].reshape((map_rows + 1) * width, depth).astype(jnp.bfloat16)
+        x1 = here[:, 1 : width + 1, :].reshape((map_rows + 1) * width, depth).astype(jnp.bfloat16)
+        count = map_rows * width
+        total = jnp.dot(x0[:count], stem_w[0], preferred_element_type=jnp.float32)
+        total += jnp.dot(x1[:count], stem_w[1], preferred_element_type=jnp.float32)
+        total += jnp.dot(x0[width:], stem_w[2], preferred_element_type=jnp.float32)
+        total += jnp.dot(x1[width:], stem_w[3], preferred_element_type=jnp.float32)
+        found = jnp.maximum(total, 0.0).astype(jnp.bfloat16)
+        feats[dest] = found
+        middle = jnp.dot(found, down_w[...], preferred_element_type=jnp.float32)
+        middle = jnp.maximum(middle, 0.0).astype(jnp.bfloat16)
+
+        @pl.when(step < lats - 1)
+        def _():
+            out_a[dest] = middle
+            sending_a(k).start()
+
+        @pl.when(step == lats - 1)
+        def _():
+            in_a[lat] = middle
+
+        return carry
+
+    lax.fori_loop(0, lats, stem, 0)
+
+    loads[2].wait()
+    group = map_rows * width
+
+    def project(k, carry):
+        @pl.when(k > 0)
+        def _():
+            sending_a(k).wait()
+
+        source = partner(k)
+        found = jnp.dot(in_a[source], height_w[...], preferred_element_type=jnp.float32)
+        at = pl.multiple_of(source * group, group)
+        for c in range(proj_h.shape[0]):
+            proj_h[c, pl.ds(at, group), :] = found[:, 128 * c : 128 * c + 128]
+        return carry
+
+    lax.fori_loop(0, lats, project, 0)
+    beside = BLOCK // full_height
+    part_width = width // HALVES
+    home = lat * lons + lon
+    column = lon * lats + lat
+
+    def sending_b(h, step):
+        k = far_first(step // lons)
+        turn = lax.rem(step, lons)
+        to_lat, to_lon = partner(k), lax.rem(lon + turn, lons)
+        return pltpu.make_async_remote_copy(
+            src_ref=out_b.at[h, to_lat * lons + to_lon],
+            dst_ref=in_b.at[h, column],
+            send_sem=send_b.at[h, step],
+            recv_sem=recv_b.at[h, step],
+            device_id={"lat": to_lat, "lon": to_lon},
+            device_id_type=MESH,
+        )
+
+    own_step = others - lons
+
+    def columns(h, carry):
+        for b in range(part_width // beside):
+            parts = []
+            for w in range(beside):
+                at = h * part_width + b * beside + w
+                parts.append(
+                    jnp.concatenate(
+                        [
+                            proj_h[c, pl.ds(at, full_height, stride=width), :]
+                            for c in range(proj_h.shape[0])
+                        ],
+                        axis=1,
+                    )
+                )
+            mine = jnp.concatenate(parts, axis=0).astype(jnp.bfloat16)
+            out = attention(mine[:, :QK], mine[:, QK : 2 * QK], mine[:, 2 * QK :], bias_h)
+            for w in range(beside):
+                for c in range(result.shape[0]):
+                    result[c, pl.ds(b * beside + w, full_height, stride=part_width), :] = out[
+                        w * full_height : (w + 1) * full_height, 128 * c : 128 * c + 128
+                    ]
+        for c in range(result.shape[0]):
+            out_b[h, :, :, 128 * c : 128 * c + 128] = (
+                result[c].astype(jnp.bfloat16).reshape(others, own_rows * part_width, 128)
+            )
+
+        def start(step, carry):
+            sending_b(h, step).start()
+            return carry
+
+        lax.fori_loop(0, own_step, start, 0)
+        lax.fori_loop(own_step + 1, others, start, 0)
+        in_b[h, column] = out_b[h, home]
+        return carry
+
+    lax.fori_loop(0, HALVES, columns, 0)
+
+    loads[3].wait()
+
+    def rows_in(h, carry):
+        def finish(step, carry):
+            sending_b(h, step).wait()
+            return carry
+
+        lax.fori_loop(0, own_step, finish, 0)
+        lax.fori_loop(own_step + 1, others, finish, 0)
+        found = jnp.dot(
+            in_b[h].reshape(others * own_rows * part_width, VD),
+            width_w[...],
+            preferred_element_type=jnp.float32,
+        ).reshape(others, own_rows, part_width, 2 * QK + VD)
+        for r in range(own_rows):
+            proj_w[r, :, h] = found[:, r]
+        return carry
+
+    lax.fori_loop(0, HALVES, rows_in, 0)
+
+    def sending_c(r, k):
+        there = lax.rem(lon + k, lons)
+        return pltpu.make_async_remote_copy(
+            src_ref=out_c.at[r, there],
+            dst_ref=in_c.at[lon, r],
+            send_sem=send_c.at[r, k],
+            recv_sem=recv_c.at[r, k],
+            device_id={"lat": lat, "lon": there},
+            device_id_type=MESH,
+        )
+
+    def row(r, carry):
+        mine = proj_w[r].reshape(full_width, 2 * QK + VD).astype(jnp.bfloat16)
+        out = attention(mine[:, :QK], mine[:, QK : 2 * QK], mine[:, 2 * QK :], bias_w)
+        out_c[r] = jnp.maximum(out, 0.0).astype(jnp.bfloat16).reshape(lons, map_cols, VD)
+
+        def start(k, carry):
+            sending_c(r, k).start()
+            return carry
+
+        lax.fori_loop(1, lons, start, 0)
+        in_c[lon, r] = out_c[r, lon]
+        return carry
+
+    lax.fori_loop(0, own_rows, row, 0)
+
+    loads[4].wait()
+
+    def widen(k, carry):
+        source = lax.rem(lon + lons - k, lons)
+
+        @pl.when(k > 0)
+        def _():
+            for r in range(own_rows):
+                sending_c(r, k).wait()
+
+        x = in_c[source].reshape(own_rows * map_cols, VD)
+        branch = jnp.dot(x, up_w[...], preferred_element_type=jnp.float32)
+        for r in range(own_rows):
+            for g in range(lats):
+                at = pl.multiple_of((source * own_rows + r) * width, width)
+                start = r * map_cols + g * width
+                total = feats[g, pl.ds(at, width), :].astype(jnp.float32)
+                total = jnp.maximum(total + branch[start : start + width], 0.0)
+                out_ref[source * own_rows + r, g * width : (g + 1) * width, :] = total.astype(
+                    jnp.bfloat16
+                )
+        return carry
+
+    lax.fori_loop(0, lons, widen, 0)
+
+
+def with_kernel(
+    imagery, stem_weight, down_weight, height_qkv, height_bias, width_qkv, width_bias, up_weight
+):
+    lats, lons = lax.axis_size("lat"), lax.axis_size("lon")
+    bf16, f32 = jnp.bfloat16, jnp.float32
+    _, rows, cols = imagery.shape
+    map_rows, map_cols = rows // PATCH, cols // PATCH
+    positions = map_rows * map_cols
+    depth, channels = stem_weight.shape[1:]
+    full_width = map_cols * lons
+    part_width = map_cols // lats // HALVES
+    own_rows = map_rows // lons
+    others = lats * lons
+    qkv = 2 * QK + VD
+    dma = pltpu.SemaphoreType.DMA
+    exchange_a = pltpu.VMEM((lats, positions // lats, VD), bf16)
+    exchange_b = pltpu.VMEM((HALVES, others, own_rows * part_width, VD), bf16)
+    return pl.pallas_call(
+        functools.partial(block_kernel, lats, lons),
+        name="block",
+        out_shape=jax.ShapeDtypeStruct((map_rows, map_cols, channels), bf16),
+        in_specs=[ANY] * 6 + [VMEM] * 2,
+        out_specs=VMEM,
+        scratch_shapes=[
+            pltpu.VMEM((3, rows + 32, cols + 256), bf16),
+            pltpu.VMEM(stem_weight.shape, bf16),
+            pltpu.VMEM(down_weight.shape, bf16),
+            pltpu.VMEM(height_qkv.shape, bf16),
+            pltpu.VMEM(width_qkv.shape, bf16),
+            pltpu.VMEM(up_weight.shape, bf16),
+            pltpu.VMEM((map_rows + 1, map_cols + 8, depth), f32),
+            pltpu.VMEM((lats, positions // lats, channels), bf16),
+            pltpu.VMEM((HEADS, BLOCK), f32),
+            pltpu.VMEM((HEADS, BLOCK, BLOCK), f32),
+            pltpu.VMEM((HEADS, full_width, full_width), f32),
+            pltpu.VMEM((qkv // 128, positions, 128), f32),
+            pltpu.VMEM((VD // 128, positions // HALVES, 128), f32),
+            pltpu.VMEM((own_rows, others, HALVES, part_width, qkv), f32),
+            exchange_a,
+            exchange_a,
+            exchange_b,
+            exchange_b,
+            pltpu.VMEM((own_rows, lons, map_cols, VD), bf16),
+            pltpu.VMEM((lons, own_rows, map_cols, VD), bf16),
+            dma((6,)),
+            dma((8,)),
+            dma((8,)),
+            dma((lats,)),
+            dma((lats,)),
+            dma((HALVES, others)),
+            dma((HALVES, others)),
+            dma((own_rows, lons)),
+            dma((own_rows, lons)),
+        ],
+        compiler_params=pltpu.CompilerParams(
+            collective_id=0, has_side_effects=True, vmem_limit_bytes=VMEM_BYTES
+        ),
+    )(
+        imagery, stem_weight, down_weight, height_qkv, width_qkv, up_weight, height_bias, width_bias
+    )
+
+
+def either(*args):
+    lats, lons = lax.axis_size("lat"), lax.axis_size("lon")
+    _, rows, cols = args[0].shape
+    map_rows, map_cols = rows // PATCH, cols // PATCH
+    height, width = map_rows * lats, map_cols // lats
+    whole_tiles = (
+        lats & (lats - 1) == 0
+        and map_cols % (16 * lats) == 0
+        and map_rows % lons == 0
+        and 2 * height - 1 <= BLOCK
+        and BLOCK % height == 0
+        and width % (8 * HALVES) == 0
+        and (width // HALVES) % (BLOCK // height) == 0
+        and (map_rows // lons) * (width // HALVES) % 16 == 0
+        and cols % 128 == 0
+        and map_rows % 8 == 0
+    )
+    return with_kernel(*args) if whole_tiles else on_device(*args)
+
+
 def solution(mesh):
     placed = (P("batch", "lat", "lon"), P(), P(), P(), P(), P(), P(), P())
     return jax.shard_map(
-        on_device,
+        either,
         mesh=mesh,
         in_specs=placed,
         out_specs=P(("batch", "lat"), "lon", None),

time: 250 us -> 57.7 us (0.23)
  local copies, waits for them, and re-layouts: 116 us -> 2.26 us
  waiting for transfers between devices: 66.6 us -> 0 us
  Pallas kernels: 0 us -> 55.2 us
  matrix products: 41.2 us -> 0 us
  between operations: 13.5 us -> 0.01 us
  starting transfers between devices: 9.32 us -> 0 us
  other arithmetic: 3.35 us -> 0 us
    gather x4 -> x0, local copies, waits for them, and re-layouts: 60.7 us -> none  [the longest x2 59.9 us: on_device(): scores = scores + jnp.take(width_bias, offsets, axis=1)[:, None]]
    all_gather x4 -> x0, waiting for transfers between devices: 56.7 us -> none  [the longest x1 32.4 us: on_device(): lax.all_gather(height_proj[..., 2 * QK:], 'lat', axis=0, tiled=True)]
    pallas_call x0 -> x1, Pallas kernels: none -> 55.2 us  [with_kernel(): pl.pallas_call(functools.partial(block_kernel, lats, lons), name='block',...]
    dot_general x11 -> x0, matrix products: 41.2 us -> none  [the longest x4 15.8 us: stem_features(): jnp.dot(window, stem_weight[2 * row_shift + col_shift], preferred_element...]
    reshape x4 -> x0, local copies, waits for them, and re-layouts: 20 us -> none  [the longest x1 6.77 us: stem_features(): blocks = padded.reshape(channels, map_rows + 1, PATCH, map_cols + 1, PATCH)]
    slice x11 -> x0, local copies, waits for them, and re-layouts: 11 us -> none  [the longest x5 8.17 us: stem_features(): blocks[row_shift:row_shift + map_rows, col_shift:col_shift + map_cols]]
    ppermute x4 -> x0, waiting for transfers between devices: 9.83 us -> none  [the longest x2 5.92 us: extended(): lax.ppermute(head, axis, [((i + 1) % count, i) for i in range(ends)])]
    ppermute x4 -> x0, starting transfers between devices: 8.79 us -> none  [the longest x2 6.47 us: extended(): lax.ppermute(tail, axis, [(i, (i + 1) % count) for i in range(ends)])]
  transfers between devices with their start and end apart: 8 -> 0, of which waited for: 6 -> 0; matrix products, arithmetic and copies ran while one was open for 33% -> 0% of each run, Pallas kernels for 0% -> 0%
where the time goes in v2:
time: 57.7 us; the launch traced here: 57.5 us
  Pallas kernels  55.2 us (96%)
  local copies, waits for them, and re-layouts  2.26 us (4%)
    pallas_call x1, Pallas kernels, with_kernel(): pl.pallas_call(functools.partial(block_kernel, lats, lons), name='block',...  55.2 us
    unnamed x1, local copies, waits for them, and re-layouts  2.26 us

profile of v2, /device:TPU:0, one launch (start us, length us, event | category | flops | bytes accessed | tf_op | source)
XLA Modules:
  0.0 57.5 jit_solution(9565795401281236947)
XLA Ops:
  0.0 55.2 %block.1 = bf16[8,64,1024]{2,1,0:T(8,128)(2,1)} custom-call(bf16[3,128,1024]{2,1,0:T(8,128)(2,1)} %img.1, bf16[4,768,1024]{2,1,0:T(8,128)(2,1)} %stem_hbm.1, bf16[1024,512]{1,0:T(8,128)(2,1)} %down_hbm.1, bf16[512,1024]{1,0:T(8,128)(2,1)} %height_hbm.1, bf16[512,1024]{1,0:T(8,128)(2,1)} %width_hbm.1, bf16[512,1024]{1,0:T(8,128)(2,1)} %up_hbm.1, ...), custom_call_target="tpu_custom_call" | custom-call | tf_op jit(solution)/shard_map/block/pallas_call | solution.py:563
  55.2 2.3 %copy.10 = bf16[8,64,1024]{2,1,0:T(8,128)(2,1)} copy(bf16[8,64,1024]{2,1,0:T(8,128)(2,1)} %block.1) | data formatting | bytes 2097152

commit v3 on v2

--- a/solution.py
+++ b/solution.py
@@ -202,7 +202,7 @@
 def block_kernel(
     lats, lons, img, stem_hbm, down_hbm, height_hbm, width_hbm, up_hbm, height_bias, width_bias,
     out_ref,
-    ext, stem_w, down_w, height_w, width_w, up_w, xs, feats, padded_bias, bias_h, bias_w,
+    ext, edge_out, edge_in, rim_out, rim_in, stem_w, down_w, height_w, width_w, up_w, xs, feats, padded_bias, bias_h, bias_w,
     proj_h, result, proj_w, out_a, in_a, out_b, in_b, out_c, in_c,
     load_sems, halo_send, halo_recv, send_a, recv_a, send_b, recv_b, send_c, recv_c,
 ):
@@ -248,22 +248,47 @@
 
     @pl.when(lat == 0)
     def _():
-        ext[:, 0:16, :] = jnp.zeros((3, 16, cols + 256), ext.dtype)
+        rim_in[0] = jnp.zeros(rim_in.shape[1:], rim_in.dtype)
+        edge_in[:, 0:16, :] = jnp.zeros((2, 16, 128), edge_in.dtype)
 
     @pl.when(lat == lats - 1)
     def _():
-        ext[:, rows + 16 : rows + 32, :] = jnp.zeros((3, 16, cols + 256), ext.dtype)
-
-    row_moves = {-1: (0, rows + 16, 16), 0: (0, 16, rows), 1: (rows - 16, 0, 16)}
-    col_moves = {-1: (0, cols + 128, 128), 0: (0, 128, cols), 1: (cols - 128, 0, 128)}
+        rim_in[1] = jnp.zeros(rim_in.shape[1:], rim_in.dtype)
+        edge_in[:, rows + 16 : rows + 32, :] = jnp.zeros((2, 16, 128), edge_in.dtype)
+
+    local.wait()
+    edge_lane = lax.broadcasted_iota(jnp.int32, (rows, 128), 1) // 8
+    for side, at in ((0, 128), (1, cols)):
+        packed = jnp.zeros((rows, 128), jnp.float32)
+        for c in range(3):
+            tile = ext[c, 16 : 16 + rows, at : at + 128].astype(jnp.float32)
+            shift = 8 * c + 8 * side
+            tile = pltpu.roll(tile, shift, 1) if shift else tile
+            packed = jnp.where(edge_lane == c, tile, packed)
+        edge_out[side] = packed.astype(jnp.bfloat16)
+    half_row = cols // 2
+    for side, at in ((0, 16), (1, rows)):
+        for c in range(3):
+            slab = ext[c, at : at + 16, 128 : 128 + cols].astype(jnp.float32)
+            slab = slab[8 * side : 8 * side + 8]
+            slab = jnp.concatenate([slab[:, :half_row], slab[:, half_row:]], axis=0)
+            rim_out[side, c] = slab.astype(jnp.bfloat16)
+
     copies = []
-    for down, right in ((-1, 0), (1, 0), (0, -1), (0, 1), (-1, -1), (-1, 1), (1, -1), (1, 1)):
-        y_from, y_to, y_size = row_moves[down]
-        x_from, x_to, x_size = col_moves[right]
+    for down, right in ((0, -1), (0, 1), (-1, 0), (1, 0), (-1, -1), (-1, 1), (1, -1), (1, 1)):
         slot = len(copies)
+        if right == 0:
+            source = rim_out.at[(1 + down) // 2]
+            target = rim_in.at[(1 - down) // 2]
+        else:
+            y_from, y_to, y_size = {
+                -1: (0, rows + 16, 16), 0: (0, 16, rows), 1: (rows - 16, 0, 16)
+            }[down]
+            source = edge_out.at[(1 + right) // 2, pl.ds(y_from, y_size), :]
+            target = edge_in.at[(1 - right) // 2, pl.ds(y_to, y_size), :]
         copy = pltpu.make_async_remote_copy(
-            src_ref=img.at[:, pl.ds(y_from, y_size), pl.ds(x_from, x_size)],
-            dst_ref=ext.at[:, pl.ds(y_to, y_size), pl.ds(x_to, x_size)],
+            src_ref=source,
+            dst_ref=target,
             send_sem=halo_send.at[slot],
             recv_sem=halo_recv.at[slot],
             device_id={
@@ -273,14 +298,6 @@
             device_id_type=MESH,
         )
         copies.append((down, copy))
-    pl.semaphore_wait(barrier, others - 1)
-    for down, copy in copies:
-        if down == 0:
-            copy.start()
-        elif down == -1:
-            pl.when(lat > 0)(copy.start)
-        else:
-            pl.when(lat < lats - 1)(copy.start)
 
     lane = lax.broadcasted_iota(jnp.int32, (8, 128), 1)
     sub = lax.broadcasted_iota(jnp.int32, (8, 128), 0)
@@ -313,8 +330,15 @@
         patch(i, tiles - 1, 1)
         return carry
 
-    local.wait()
     lax.fori_loop(1, map_rows, inner, 0)
+    pl.semaphore_wait(barrier, others - 1)
+    for down, copy in copies:
+        if down == 0:
+            copy.start()
+        elif down == -1:
+            pl.when(lat > 0)(copy.start)
+        else:
+            pl.when(lat < lats - 1)(copy.start)
 
     padded_bias[...] = jnp.zeros(padded_bias.shape, jnp.float32)
     padded_bias[:, 0 : height_bias.shape[1]] = height_bias[...]
@@ -337,6 +361,20 @@
         else:
             pl.when(lat < lats - 1)(copy.wait_send)
             pl.when(lat > 0)(copy.wait_recv)
+    for c in range(3):
+        for side, at in ((0, 0), (1, cols + 128)):
+            tile = edge_in[side].astype(jnp.float32)
+            shift = (128 - 8 * c - 8 * (1 - side)) % 128
+            tile = pltpu.roll(tile, shift, 1) if shift else tile
+            ext[c, :, at : at + 128] = tile.astype(jnp.bfloat16)
+        for side, at in ((0, 0), (1, rows + 16)):
+            slab = rim_in[side, c].astype(jnp.float32)
+            slab = jnp.concatenate([slab[:8], slab[8:]], axis=1)
+            blank = jnp.zeros_like(slab)
+            slab = [blank, slab] if side == 0 else [slab, blank]
+            ext[c, at : at + 16, 128 : 128 + cols] = jnp.concatenate(slab, axis=0).astype(
+                jnp.bfloat16
+            )
     patch(0, 1, tiles - 2)
     patch(map_rows, 1, tiles - 2)
     lax.fori_loop(0, map_rows + 1, rim, 0)
@@ -357,65 +395,64 @@
             bit *= 2
         return other
 
-    def sending_a(k):
+    part_width = width // HALVES
+    count = map_rows * part_width
+
+    def sending_a(h, k):
         dest = partner(k)
         return pltpu.make_async_remote_copy(
-            src_ref=out_a.at[dest],
-            dst_ref=in_a.at[lat],
-            send_sem=send_a.at[k],
-            recv_sem=recv_a.at[k],
+            src_ref=out_a.at[h, dest],
+            dst_ref=in_a.at[h, lat],
+            send_sem=send_a.at[h, k],
+            recv_sem=recv_a.at[h, k],
             device_id={"lat": dest, "lon": lon},
             device_id_type=MESH,
         )
 
     def stem(step, carry):
-        k = far_first(step)
-        dest = partner(k)
-        first = pl.multiple_of(dest * width, width)
-        here = xs[:, pl.ds(first, width + 8), :]
-        x0 = here[:, :width, :].reshape((map_rows + 1) * width, depth).astype(jnp.bfloat16)
-        x1 = here[:, 1 : width + 1, :].reshape((map_rows + 1) * width, depth).astype(jnp.bfloat16)
-        count = map_rows * width
-        total = jnp.dot(x0[:count], stem_w[0], preferred_element_type=jnp.float32)
-        total += jnp.dot(x1[:count], stem_w[1], preferred_element_type=jnp.float32)
-        total += jnp.dot(x0[width:], stem_w[2], preferred_element_type=jnp.float32)
-        total += jnp.dot(x1[width:], stem_w[3], preferred_element_type=jnp.float32)
+        h = step // (lats // 2)
+        ks = [far_first(2 * lax.rem(step, lats // 2) + n) for n in range(2)]
+        dests = [partner(k) for k in ks]
+        blocks = [[], [], [], []]
+        for dest in dests:
+            first = pl.multiple_of(dest * width + h * part_width, part_width)
+            here = xs[:, pl.ds(first, part_width + 8), :]
+            for shift in range(2):
+                x = here[:, shift : shift + part_width, :]
+                x = x.reshape((map_rows + 1) * part_width, depth)
+                blocks[shift].append(x[:count].astype(jnp.bfloat16))
+                blocks[2 + shift].append(x[part_width:].astype(jnp.bfloat16))
+        total = jnp.zeros((2 * count, stem_w.shape[2]), jnp.float32)
+        for quadrant in range(4):
+            total += jnp.dot(
+                jnp.concatenate(blocks[quadrant], axis=0),
+                stem_w[quadrant],
+                preferred_element_type=jnp.float32,
+            )
         found = jnp.maximum(total, 0.0).astype(jnp.bfloat16)
-        feats[dest] = found
         middle = jnp.dot(found, down_w[...], preferred_element_type=jnp.float32)
         middle = jnp.maximum(middle, 0.0).astype(jnp.bfloat16)
-
-        @pl.when(step < lats - 1)
-        def _():
-            out_a[dest] = middle
-            sending_a(k).start()
-
-        @pl.when(step == lats - 1)
-        def _():
-            in_a[lat] = middle
-
-        return carry
-
-    lax.fori_loop(0, lats, stem, 0)
+        for n in range(2):
+            k, dest = ks[n], dests[n]
+            mine = middle[n * count : (n + 1) * count]
+
+            @pl.when(k > 0)
+            def _():
+                out_a[h, dest] = mine
+                sending_a(h, k).start()
+
+            @pl.when(k == 0)
+            def _():
+                in_a[h, lat] = mine
+
+        for n in range(2):
+            feats[dests[n], h] = found[n * count : (n + 1) * count].astype(jnp.float32)
+        return carry
+
+    lax.fori_loop(0, HALVES * lats // 2, stem, 0)
 
     loads[2].wait()
-    group = map_rows * width
-
-    def project(k, carry):
-        @pl.when(k > 0)
-        def _():
-            sending_a(k).wait()
-
-        source = partner(k)
-        found = jnp.dot(in_a[source], height_w[...], preferred_element_type=jnp.float32)
-        at = pl.multiple_of(source * group, group)
-        for c in range(proj_h.shape[0]):
-            proj_h[c, pl.ds(at, group), :] = found[:, 128 * c : 128 * c + 128]
-        return carry
-
-    lax.fori_loop(0, lats, project, 0)
     beside = BLOCK // full_height
-    part_width = width // HALVES
     home = lat * lons + lon
     column = lon * lats + lat
 
@@ -435,14 +472,24 @@
     own_step = others - lons
 
     def columns(h, carry):
+        def arrived(k, carry):
+            sending_a(h, k).wait()
+            return carry
+
+        lax.fori_loop(1, lats, arrived, 0)
+        found = jnp.dot(
+            in_a[h].reshape(lats * count, VD), height_w[...], preferred_element_type=jnp.float32
+        )
+        for c in range(proj_h.shape[0]):
+            proj_h[c] = found[:, 128 * c : 128 * c + 128]
         for b in range(part_width // beside):
             parts = []
             for w in range(beside):
-                at = h * part_width + b * beside + w
+                at = b * beside + w
                 parts.append(
                     jnp.concatenate(
                         [
-                            proj_h[c, pl.ds(at, full_height, stride=width), :]
+                            proj_h[c, pl.ds(at, full_height, stride=part_width), :]
                             for c in range(proj_h.shape[0])
                         ],
                         axis=1,
@@ -530,14 +577,13 @@
         x = in_c[source].reshape(own_rows * map_cols, VD)
         branch = jnp.dot(x, up_w[...], preferred_element_type=jnp.float32)
         for r in range(own_rows):
-            for g in range(lats):
-                at = pl.multiple_of((source * own_rows + r) * width, width)
-                start = r * map_cols + g * width
-                total = feats[g, pl.ds(at, width), :].astype(jnp.float32)
-                total = jnp.maximum(total + branch[start : start + width], 0.0)
-                out_ref[source * own_rows + r, g * width : (g + 1) * width, :] = total.astype(
-                    jnp.bfloat16
-                )
+            i = source * own_rows + r
+            at = pl.multiple_of(i * part_width, part_width)
+            kept = [
+                feats[g, h, pl.ds(at, part_width), :] for g in range(lats) for h in range(HALVES)
+            ]
+            total = jnp.concatenate(kept, axis=0) + branch[r * map_cols : (r + 1) * map_cols]
+            out_ref[i] = jnp.maximum(total, 0.0).astype(jnp.bfloat16)
         return carry
 
     lax.fori_loop(0, lons, widen, 0)
@@ -558,7 +604,7 @@
     others = lats * lons
     qkv = 2 * QK + VD
     dma = pltpu.SemaphoreType.DMA
-    exchange_a = pltpu.VMEM((lats, positions // lats, VD), bf16)
+    exchange_a = pltpu.VMEM((HALVES, lats, map_rows * part_width, VD), bf16)
     exchange_b = pltpu.VMEM((HALVES, others, own_rows * part_width, VD), bf16)
     return pl.pallas_call(
         functools.partial(block_kernel, lats, lons),
@@ -568,17 +614,21 @@
         out_specs=VMEM,
         scratch_shapes=[
             pltpu.VMEM((3, rows + 32, cols + 256), bf16),
+            pltpu.VMEM((2, rows, 128), bf16),
+            pltpu.VMEM((2, rows + 32, 128), bf16),
+            pltpu.VMEM((2, 3, 16, cols // 2), bf16),
+            pltpu.VMEM((2, 3, 16, cols // 2), bf16),
             pltpu.VMEM(stem_weight.shape, bf16),
             pltpu.VMEM(down_weight.shape, bf16),
             pltpu.VMEM(height_qkv.shape, bf16),
             pltpu.VMEM(width_qkv.shape, bf16),
             pltpu.VMEM(up_weight.shape, bf16),
             pltpu.VMEM((map_rows + 1, map_cols + 8, depth), f32),
-            pltpu.VMEM((lats, positions // lats, channels), bf16),
+            pltpu.VMEM((lats, HALVES, map_rows * part_width, channels), f32),
             pltpu.VMEM((HEADS, BLOCK), f32),
             pltpu.VMEM((HEADS, BLOCK, BLOCK), f32),
             pltpu.VMEM((HEADS, full_width, full_width), f32),
-            pltpu.VMEM((qkv // 128, positions, 128), f32),
+            pltpu.VMEM((qkv // 128, positions // HALVES, 128), f32),
             pltpu.VMEM((VD // 128, positions // HALVES, 128), f32),
             pltpu.VMEM((own_rows, others, HALVES, part_width, qkv), f32),
             exchange_a,
@@ -590,8 +640,8 @@
             dma((6,)),
             dma((8,)),
             dma((8,)),
-            dma((lats,)),
-            dma((lats,)),
+            dma((HALVES, lats)),
+            dma((HALVES, lats)),
             dma((HALVES, others)),
             dma((HALVES, others)),
             dma((own_rows, lons)),
@@ -612,6 +662,10 @@
     height, width = map_rows * lats, map_cols // lats
     whole_tiles = (
         lats & (lats - 1) == 0
+        and lats > 1
+        and rows % 16 == 0
+        and cols % 256 == 0
+        and map_rows * (width // HALVES) % 16 == 0
         and map_cols % (16 * lats) == 0
         and map_rows % lons == 0
         and 2 * height - 1 <= BLOCK

time: 57.7 us -> 54.9 us (0.951)
  Pallas kernels: 55.2 us -> 52.4 us
    pallas_call x1, Pallas kernels: 55.2 us -> 52.4 us  [with_kernel(): pl.pallas_call(functools.partial(block_kernel, lats, lons), name='block',...]
where the time goes in v3:
time: 54.9 us; the launch traced here: 54.7 us
  Pallas kernels  52.4 us (95%)
  local copies, waits for them, and re-layouts  2.26 us (4%)
    pallas_call x1, Pallas kernels, with_kernel(): pl.pallas_call(functools.partial(block_kernel, lats, lons), name='block',...  52.4 us
    unnamed x1, local copies, waits for them, and re-layouts  2.26 us

profile of v3, /device:TPU:0, one launch (start us, length us, event | category | flops | bytes accessed | tf_op | source)
XLA Modules:
  0.0 54.7 jit_solution(652728782995380639)
XLA Ops:
  0.0 52.4 %block.1 = bf16[8,64,1024]{2,1,0:T(8,128)(2,1)} custom-call(bf16[3,128,1024]{2,1,0:T(8,128)(2,1)} %img.1, bf16[4,768,1024]{2,1,0:T(8,128)(2,1)} %stem_hbm.1, bf16[1024,512]{1,0:T(8,128)(2,1)} %down_hbm.1, bf16[512,1024]{1,0:T(8,128)(2,1)} %height_hbm.1, bf16[512,1024]{1,0:T(8,128)(2,1)} %width_hbm.1, bf16[512,1024]{1,0:T(8,128)(2,1)} %up_hbm.1, ...), custom_call_target="tpu_custom_call" | custom-call | tf_op jit(solution)/shard_map/block/pallas_call | solution.py:609
  52.4 2.3 %copy.10 = bf16[8,64,1024]{2,1,0:T(8,128)(2,1)} copy(bf16[8,64,1024]{2,1,0:T(8,128)(2,1)} %block.1) | data formatting | bytes 2097152

commit v4 on v3

--- a/solution.py
+++ b/solution.py
@@ -166,12 +166,6 @@
 HALVES = 2
 VMEM_BYTES = 58 * 1024 * 1024
 LOG2E = 1.4426950408889634
-
-
-def chunks_turned(tile, to_bands, pick, to_rows):
-    turned = jnp.take_along_axis(tile, to_bands, axis=1, mode="promise_in_bounds")
-    turned = jnp.take_along_axis(turned, pick, axis=0, mode="promise_in_bounds")
-    return jnp.take_along_axis(turned, to_rows, axis=1, mode="promise_in_bounds")
 
 
 def attention(q, k, v, bias):
@@ -304,6 +298,8 @@
     to_bands = lax.rem(lane - 16 * sub + 128, 128)
     pick = lax.rem(lane // 16 - sub + 8, 8)
     to_rows = lax.rem(lane + 16 * sub, 128)
+    from_bands = lax.rem(to_bands + 120, 128)
+    taken = functools.partial(jnp.take_along_axis, mode="promise_in_bounds")
     tiles = cols // 128 + 1
 
     def patch(i, first, count):
@@ -314,11 +310,15 @@
                 128 * first : 128 * (first + count + 1),
             ].astype(jnp.float32)
             for half in range(2):
-                part = slab[8 + 8 * half : 16 + 8 * half, 120 : 120 + 128 * count]
+                part = slab[8 + 8 * half : 16 + 8 * half]
+                bands = [
+                    taken(part[:, 128 * t : 128 * t + 128], from_bands, axis=1) for t in range(count + 1)
+                ]
                 for t in range(count):
                     at = 8 * (first + t)
-                    xs[i, at : at + 8, (2 * c + half) * 128 : (2 * c + half + 1) * 128] = (
-                        chunks_turned(part[:, 128 * t : 128 * t + 128], to_bands, pick, to_rows)
+                    tile = taken(jnp.where(to_bands < 8, bands[t], bands[t + 1]), pick, axis=0)
+                    xs[i, at : at + 8, (2 * c + half) * 128 : (2 * c + half + 1) * 128] = taken(
+                        tile, to_rows, axis=1
                     )
 
     def inner(i, carry):
@@ -330,7 +330,6 @@
         patch(i, tiles - 1, 1)
         return carry
 
-    lax.fori_loop(1, map_rows, inner, 0)
     pl.semaphore_wait(barrier, others - 1)
     for down, copy in copies:
         if down == 0:
@@ -339,6 +338,8 @@
             pl.when(lat > 0)(copy.start)
         else:
             pl.when(lat < lats - 1)(copy.start)
+
+    lax.fori_loop(1, map_rows, inner, 0)
 
     padded_bias[...] = jnp.zeros(padded_bias.shape, jnp.float32)
     padded_bias[:, 0 : height_bias.shape[1]] = height_bias[...]

time: 54.9 us -> 51.7 us (0.942)
  Pallas kernels: 52.4 us -> 49.1 us
    pallas_call x1, Pallas kernels: 52.4 us -> 49.1 us  [with_kernel(): pl.pallas_call(functools.partial(block_kernel, lats, lons), name='block',...]
where the time goes in v4:
time: 51.7 us; the launch traced here: 51.4 us
  Pallas kernels  49.1 us (95%)
  local copies, waits for them, and re-layouts  2.26 us (4%)
    pallas_call x1, Pallas kernels, with_kernel(): pl.pallas_call(functools.partial(block_kernel, lats, lons), name='block',...  49.1 us
    unnamed x1, local copies, waits for them, and re-layouts  2.26 us

profile of v4, /device:TPU:0, one launch (start us, length us, event | category | flops | bytes accessed | tf_op | source)
XLA Modules:
  0.0 51.4 jit_solution(4150523940367691285)
XLA Ops:
  0.0 49.1 %block.1 = bf16[8,64,1024]{2,1,0:T(8,128)(2,1)} custom-call(bf16[3,128,1024]{2,1,0:T(8,128)(2,1)} %img.1, bf16[4,768,1024]{2,1,0:T(8,128)(2,1)} %stem_hbm.1, bf16[1024,512]{1,0:T(8,128)(2,1)} %down_hbm.1, bf16[512,1024]{1,0:T(8,128)(2,1)} %height_hbm.1, bf16[512,1024]{1,0:T(8,128)(2,1)} %width_hbm.1, bf16[512,1024]{1,0:T(8,128)(2,1)} %up_hbm.1, ...), custom_call_target="tpu_custom_call" | custom-call | tf_op jit(solution)/shard_map/block/pallas_call | solution.py:610
  49.1 2.3 %copy.10 = bf16[8,64,1024]{2,1,0:T(8,128)(2,1)} copy(bf16[8,64,1024]{2,1,0:T(8,128)(2,1)} %block.1) | data formatting | bytes 2097152
